TPU v7x, 32 devices: a whole 2x2x4 slice. The times are simulated.
32 devices in a mesh: cohort: 2 (over x), ind: 16 (over z, y, core).
Axes of the slice: x: 2, y: 2, z: 4, core: 2. Of those that a mesh axis runs over, the one named last changes fastest.
Arguments:
- genotypes: float32 [65536, 1200], P(('cohort', 'ind')), parts along dimension 0, may hold values from -6.5 to 6.5
- solution: float32 [16, 65536], P(None, ('cohort', 'ind')), parts along dimension 1, may hold values from -6 to 6
- residual: float32 [16, 65536], P(None, ('cohort', 'ind')), parts along dimension 1, may hold values from -6 to 6
- direction: float32 [16, 65536], P(None, ('cohort', 'ind')), parts along dimension 1, may hold values from -6 to 6
- ratio: float32 [32], P('cohort'), parts along dimension 0, may hold values from 0.2 to 5
Outputs:
- solution_out: float32 [16, 65536], P(None, ('cohort', 'ind')), parts along dimension 1
- residual_out: float32 [16, 65536], P(None, ('cohort', 'ind')), parts along dimension 1
- direction_out: float32 [16, 65536], P(None, ('cohort', 'ind')), parts along dimension 1
There are 2 independent parts, one for each index of `cohort`. A program takes and returns all parts, laid end to end along the dimension named above; each array names one. Nothing has to cross between parts.
All inputs are finite; a program needn't handle non-finite values.
Results may differ from a plain program's by a relative error of at most 0.0003.
Values sent between devices are 32-bit elements; how exact they have to be, the bound alone decides.
A program may use at most 64 MiB of HBM per device.

v0:
```python
import jax
import jax.numpy as jnp
from jax import lax
from jax.sharding import PartitionSpec as P

ITERS = 8


def squares(residual):
    return lax.psum(jnp.sum(residual * residual, axis=1), "ind")


def sum_over_people(values):
    return lax.psum(values, "ind")


def per_device(genotypes, solution, residual, direction, ratio):
    snps = genotypes.shape[1]
    norm_now = squares(residual)
    for step in range(ITERS):
        partial_sums = jnp.dot(
            direction,
            genotypes,
            precision=lax.Precision.HIGHEST,
            preferred_element_type=jnp.float32,
        )
        snp_sums = sum_over_people(partial_sums)
        back = lax.dot_general(
            snp_sums,
            genotypes,
            (((1,), (1,)), ((), ())),
            precision=lax.Precision.HIGHEST,
            preferred_element_type=jnp.float32,
        )
        image = back / snps + ratio[:, None] * direction
        curvature = lax.psum(jnp.sum(direction * image, axis=1), "ind")
        alpha = norm_now / curvature
        solution = solution + alpha[:, None] * direction
        residual = residual - alpha[:, None] * image
        fresh = squares(residual)
        direction = residual + (fresh / norm_now)[:, None] * direction
        norm_now = fresh
    return (solution, residual, direction)


def solution(mesh):
    in_specs = (
        P(("cohort", "ind"), None),
        P(None, ("cohort", "ind")),
        P(None, ("cohort", "ind")),
        P(None, ("cohort", "ind")),
        P("cohort"),
    )
    out_specs = (P(None, ("cohort", "ind")), P(None, ("cohort", "ind")), P(None, ("cohort", "ind")))
    return jax.shard_map(
        per_device, mesh=mesh, in_specs=in_specs, out_specs=out_specs, check_vma=False
    )
```

profile of v0, /device:TPU:0, one launch (start us, length us, event | category | flops | bytes accessed | tf_op | source)
XLA Modules:
  0.0 1330.2 jit_solution(2106268259727655599)
XLA Ops:
  7.2 12.5 fusion.8
  20.0 87.8 %all-reduce.10.cloned.1.call-done = f32[16,1200]{1,0:T(8,128)} async-done(((f32[16,1200]{1,0:T(8,128)}), f32[16,1200]{1,0:T(8,128)}) %all-reduce.10.cloned.1.call-update) | async-done | bytes 76816 | tf_op jit(solution)/shard_map/psum | solution.py:14
  107.8 7.4 multiply_reduce_fusion.15
  115.2 32.4 %all-reduce = (f32[16]{0:T(128)S(1)}, f32[16]{0:T(128)S(1)}) all-reduce(f32[16]{0:T(128)S(1)} %multiply_reduce_fusion.16, f32[16]{0:T(128)S(1)} %get-tuple-element.23), channel_id=1, replica_groups=mesh['cohort'=2,'ind'=16] {'ind'}, use_global_device_ids=true, to_apply=%region_1.0 | all-reduce | flops 32 | bytes 256 | tf_op jit(solution)/shard_map/psum | solution.py:10
  147.8 30.0 %psum.178 = f32[16]{0:T(128)S(1)} all-reduce(f32[16]{0:T(128)S(1)} %get-tuple-element.19), channel_id=1, replica_groups=mesh['cohort'=2,'ind'=16] {'ind'}, use_global_device_ids=true, to_apply=%region_6.0 | all-reduce | flops 16 | bytes 128 | tf_op jit(solution)/shard_map/psum | solution.py:10
  177.9 11.2 fusion.9
  189.2 82.5 %all-reduce.12.cloned.1.call-done = f32[16,1200]{1,0:T(8,128)} async-done(((f32[16,1200]{1,0:T(8,128)}), f32[16,1200]{1,0:T(8,128)}) %all-reduce.12.cloned.1.call-update) | async-done | bytes 76816 | tf_op jit(solution)/shard_map/psum | solution.py:14
  271.7 7.4 multiply_reduce_fusion.13
  279.0 32.4 %psum.180 = f32[16]{0:T(128)S(1)} all-reduce(f32[16]{0:T(128)S(1)} %get-tuple-element.25), channel_id=1, replica_groups=mesh['cohort'=2,'ind'=16] {'ind'}, use_global_device_ids=true, to_apply=%region_9.0 | all-reduce | flops 16 | bytes 128 | tf_op jit(solution)/shard_map/psum | solution.py:36
  311.5 0.2 multiply_reduce_fusion.12
  311.7 29.5 %psum.181 = f32[16]{0:T(128)S(1)} all-reduce(f32[16]{0:T(128)S(1)} %get-tuple-element.17), channel_id=1, replica_groups=mesh['cohort'=2,'ind'=16] {'ind'}, use_global_device_ids=true, to_apply=%region_11.0 | all-reduce | flops 16 | bytes 128 | tf_op jit(solution)/shard_map/psum | solution.py:10
  341.3 11.2 fusion.10
  352.5 0.2 all-reduce.16.cloned.1.call-start
  352.7 82.4 %all-reduce.14.cloned.1.call-done = f32[16,1200]{1,0:T(8,128)} async-done(((f32[16,1200]{1,0:T(8,128)}), f32[16,1200]{1,0:T(8,128)}) %all-reduce.14.cloned.1.call-update) | async-done | bytes 76816 | tf_op jit(solution)/shard_map/psum | solution.py:14
  435.1 7.4 multiply_reduce_fusion.11
  442.4 32.4 %psum.183 = f32[16]{0:T(128)S(1)} all-reduce(f32[16]{0:T(128)S(1)} %get-tuple-element.27), channel_id=1, replica_groups=mesh['cohort'=2,'ind'=16] {'ind'}, use_global_device_ids=true, to_apply=%region_14.0 | all-reduce | flops 16 | bytes 128 | tf_op jit(solution)/shard_map/psum | solution.py:36
  474.8 0.2 multiply_reduce_fusion.10
  475.1 29.5 %psum.184 = f32[16]{0:T(128)S(1)} all-reduce(f32[16]{0:T(128)S(1)} %get-tuple-element.15), channel_id=1, replica_groups=mesh['cohort'=2,'ind'=16] {'ind'}, use_global_device_ids=true, to_apply=%region_16.0 | all-reduce | flops 16 | bytes 128 | tf_op jit(solution)/shard_map/psum | solution.py:10
  504.6 11.2 fusion.11
  515.9 82.5 %all-reduce.16.cloned.1.call-done = f32[16,1200]{1,0:T(8,128)} async-done(((f32[16,1200]{1,0:T(8,128)}), f32[16,1200]{1,0:T(8,128)}) %all-reduce.16.cloned.1.call-update) | async-done | bytes 76816 | tf_op jit(solution)/shard_map/psum | solution.py:14
  598.4 7.4 multiply_reduce_fusion.9
  605.8 32.4 %psum.186 = f32[16]{0:T(128)S(1)} all-reduce(f32[16]{0:T(128)S(1)} %get-tuple-element.29), channel_id=1, replica_groups=mesh['cohort'=2,'ind'=16] {'ind'}, use_global_device_ids=true, to_apply=%region_19.0 | all-reduce | flops 16 | bytes 128 | tf_op jit(solution)/shard_map/psum | solution.py:36
  638.2 0.2 multiply_reduce_fusion.8
  638.4 29.7 %psum.187 = f32[16]{0:T(128)S(1)} all-reduce(f32[16]{0:T(128)S(1)} %get-tuple-element.13), channel_id=1, replica_groups=mesh['cohort'=2,'ind'=16] {'ind'}, use_global_device_ids=true, to_apply=%region_21.0 | all-reduce | flops 16 | bytes 128 | tf_op jit(solution)/shard_map/psum | solution.py:10
  668.2 11.2 fusion.12
  679.5 82.5 %all-reduce.18.cloned.1.call-done = f32[16,1200]{1,0:T(8,128)} async-done(((f32[16,1200]{1,0:T(8,128)}), f32[16,1200]{1,0:T(8,128)}) %all-reduce.18.cloned.1.call-update) | async-done | bytes 76816 | tf_op jit(solution)/shard_map/psum | solution.py:14
  762.0 7.4 multiply_reduce_fusion.7
  769.4 32.4 %psum.189 = f32[16]{0:T(128)S(1)} all-reduce(f32[16]{0:T(128)S(1)} %get-tuple-element.31), channel_id=1, replica_groups=mesh['cohort'=2,'ind'=16] {'ind'}, use_global_device_ids=true, to_apply=%region_24.0 | all-reduce | flops 16 | bytes 128 | tf_op jit(solution)/shard_map/psum | solution.py:36
  802.0 29.5 %psum.190 = f32[16]{0:T(128)S(1)} all-reduce(f32[16]{0:T(128)S(1)} %get-tuple-element.11), channel_id=1, replica_groups=mesh['cohort'=2,'ind'=16] {'ind'}, use_global_device_ids=true, to_apply=%region_26.0 | all-reduce | flops 16 | bytes 128 | tf_op jit(solution)/shard_map/psum | solution.py:10
  831.6 11.2 fusion.13
  842.8 0.3 all-reduce.22.cloned.1.call-start
  843.1 82.3 %all-reduce.20.cloned.1.call-done = f32[16,1200]{1,0:T(8,128)} async-done(((f32[16,1200]{1,0:T(8,128)}), f32[16,1200]{1,0:T(8,128)}) %all-reduce.20.cloned.1.call-update) | async-done | bytes 76816 | tf_op jit(solution)/shard_map/psum | solution.py:14
  925.4 7.4 multiply_reduce_fusion.5
  932.7 32.4 %psum.192 = f32[16]{0:T(128)S(1)} all-reduce(f32[16]{0:T(128)S(1)} %get-tuple-element.33), channel_id=1, replica_groups=mesh['cohort'=2,'ind'=16] {'ind'}, use_global_device_ids=true, to_apply=%region_29.0 | all-reduce | flops 16 | bytes 128 | tf_op jit(solution)/shard_map/psum | solution.py:36
  965.2 0.2 multiply_reduce_fusion.4
  965.4 29.5 %psum.193 = f32[16]{0:T(128)S(1)} all-reduce(f32[16]{0:T(128)S(1)} %get-tuple-element.9), channel_id=1, replica_groups=mesh['cohort'=2,'ind'=16] {'ind'}, use_global_device_ids=true, to_apply=%region_31.0 | all-reduce | flops 16 | bytes 128 | tf_op jit(solution)/shard_map/psum | solution.py:10
  995.0 11.2 fusion.14
  1006.2 82.5 %all-reduce.22.cloned.1.call-done = f32[16,1200]{1,0:T(8,128)} async-done(((f32[16,1200]{1,0:T(8,128)}), f32[16,1200]{1,0:T(8,128)}) %all-reduce.22.cloned.1.call-update) | async-done | bytes 76816 | tf_op jit(solution)/shard_map/psum | solution.py:14
  1088.8 7.4 multiply_reduce_fusion.3
  1096.1 32.4 %psum.195 = f32[16]{0:T(128)S(1)} all-reduce(f32[16]{0:T(128)S(1)} %get-tuple-element.35), channel_id=1, replica_groups=mesh['cohort'=2,'ind'=16] {'ind'}, use_global_device_ids=true, to_apply=%region_34.0 | all-reduce | flops 16 | bytes 128 | tf_op jit(solution)/shard_map/psum | solution.py:36
  1128.6 0.2 multiply_reduce_fusion.2
  1128.8 29.8 %psum.196 = f32[16]{0:T(128)S(1)} all-reduce(f32[16]{0:T(128)S(1)} %get-tuple-element.7), channel_id=1, replica_groups=mesh['cohort'=2,'ind'=16] {'ind'}, use_global_device_ids=true, to_apply=%region_36.0 | all-reduce | flops 16 | bytes 128 | tf_op jit(solution)/shard_map/psum | solution.py:10
  1158.7 11.2 fusion.15
  1169.9 82.6 %all-reduce.24.cloned.1.call-done = f32[16,1200]{1,0:T(8,128)} async-done(((f32[16,1200]{1,0:T(8,128)}), f32[16,1200]{1,0:T(8,128)}) %all-reduce.24.cloned.1.call-update) | async-done | bytes 76816 | tf_op jit(solution)/shard_map/psum | solution.py:14
  1252.5 7.4 multiply_reduce_fusion.1
  1259.8 32.4 %psum.198 = f32[16]{0:T(128)S(1)} all-reduce(f32[16]{0:T(128)S(1)} %get-tuple-element.37), channel_id=1, replica_groups=mesh['cohort'=2,'ind'=16] {'ind'}, use_global_device_ids=true, to_apply=%region_39.0 | all-reduce | flops 16 | bytes 128 | tf_op jit(solution)/shard_map/psum | solution.py:36
  1292.5 29.5 %psum.199 = f32[16]{0:T(128)S(1)} all-reduce(f32[16]{0:T(128)S(1)} %get-tuple-element.5), channel_id=1, replica_groups=mesh['cohort'=2,'ind'=16] {'ind'}, use_global_device_ids=true, to_apply=%region_41.0 | all-reduce | flops 16 | bytes 128 | tf_op jit(solution)/shard_map/psum | solution.py:10
  1322.0 0.9 multiply_add_fusion
  (51 shorter events, 1.9 us)
Async XLA Ops:
  7.2 100.6 %copy-start = (f32[16,2048]{1,0:T(8,128)S(1)}, f32[16,2048]{1,0:T(8,128)}, u32[]{:S(2)}) copy-start(f32[16,2048]{1,0:T(8,128)} %param.8) | copy-start | bytes 393220
  7.2 12.6 copy-start.2
  7.2 100.6 %copy-start.4 = (f32[16]{0:T(128)S(1)}, f32[16]{0:T(128)}, u32[]{:S(2)}) copy-start(f32[16]{0:T(128)} %param.9) | copy-start | bytes 196
  7.2 100.6 %all-reduce.10.cloned.1.call-start = ((), (), s32[]{:S(2)}) async-start(), calls=%async_computation | async-start | bytes 163840 | tf_op jit(solution)/shard_map/psum | solution.py:14
  19.8 251.9 %all-reduce.12.cloned.1.call-start = ((), (), s32[]{:S(2)}) async-start(), calls=%async_computation.1 | async-start | bytes 163840 | tf_op jit(solution)/shard_map/psum | solution.py:14
  189.1 245.9 %all-reduce.14.cloned.1.call-start = ((), (), s32[]{:S(2)}) async-start(), calls=%async_computation.2 | async-start | bytes 163840 | tf_op jit(solution)/shard_map/psum | solution.py:14
  352.5 245.9 %all-reduce.16.cloned.1.call-start = ((), (), s32[]{:S(2)}) async-start(), calls=%async_computation.3 | async-start | bytes 163840 | tf_op jit(solution)/shard_map/psum | solution.py:14
  515.9 246.2 %all-reduce.18.cloned.1.call-start = ((), (), s32[]{:S(2)}) async-start(), calls=%async_computation.4 | async-start | bytes 163840 | tf_op jit(solution)/shard_map/psum | solution.py:14
  679.4 245.9 %all-reduce.20.cloned.1.call-start = ((), (), s32[]{:S(2)}) async-start(), calls=%async_computation.5 | async-start | bytes 163840 | tf_op jit(solution)/shard_map/psum | solution.py:14
  842.8 245.9 %all-reduce.22.cloned.1.call-start = ((), (), s32[]{:S(2)}) async-start(), calls=%async_computation.6 | async-start | bytes 163840 | tf_op jit(solution)/shard_map/psum | solution.py:14
  1006.2 246.3 %all-reduce.24.cloned.1.call-start = ((), (), s32[]{:S(2)}) async-start(), calls=%async_computation.7 | async-start | bytes 163840 | tf_op jit(solution)/shard_map/psum | solution.py:14
  1158.6 163.3 %copy-start.3 = (f32[16,2048]{1,0:T(8,128)S(1)}, f32[16,2048]{1,0:T(8,128)}, u32[]{:S(2)}) copy-start(f32[16,2048]{1,0:T(8,128)} %param.6) | copy-start | bytes 393220
  1292.5 30.4 %copy-start.1 = (f32[16,2048]{1,0:T(8,128)}, f32[16,2048]{1,0:T(8,128)S(1)}, u32[]{:S(2)}) copy-start(f32[16,2048]{1,0:T(8,128)S(1)} %get-tuple-element.6) | copy-start | bytes 393220
Sparse Core Ops, SparseCore 0:
  19.9 87.8 all-reduce.9
  189.2 82.3 all-reduce.11
  352.6 82.4 all-reduce.13
  516.0 82.3 all-reduce.15
  679.6 82.4 all-reduce.17
  842.9 82.3 all-reduce.19
  1006.3 82.4 all-reduce.21
  1170.0 82.3 all-reduce.23
where the time goes:
time: 1340 us; the launch traced here: 1330 us
  waiting for transfers between devices  665 us (50%)
  blocking collectives  496 us (37%)
  matrix products  150 us (11%)
  between operations  14.8 us (1%)
    psum x8, waiting for transfers between devices, sum_over_people(): return lax.psum(values, 'ind')  665 us
    psum x9, blocking collectives, squares(): return lax.psum(jnp.sum(residual * residual, axis=1), 'ind')  269 us
    psum x7, blocking collectives, per_device(): curvature = lax.psum(jnp.sum(direction * image, axis=1), 'ind')  227 us
    dot_general x8, matrix products, per_device(): jnp.dot(direction, genotypes, precision=lax.Precision.HIGHEST, preferred_...  90.9 us
    dot_general x8, matrix products, per_device(): lax.dot_general(snp_sums, genotypes, (((1,), (1,)), ((), ())), precision=...  59 us
  transfers between devices with their start and end apart: 8, of which 8 were waited for; matrix products, arithmetic and copies ran while one was open for 0% of the time, Pallas kernels for 0%

commit v1 on v0

v1 whole, which is shorter than its diff:
```python
import functools

import jax
import jax.numpy as jnp
from jax import lax
from jax.experimental import pallas as pl
from jax.experimental.pallas import tpu as pltpu
from jax.sharding import PartitionSpec as P

ITERS = 8
LANES = 128
F32 = jnp.float32
BF16 = jnp.bfloat16


def split(value):
    high = value.astype(BF16)
    low = (value - high.astype(F32)).astype(BF16)
    return high, low


def product(rows, w_high, w_low, transposed=False):
    dims = (((1,), (1 if transposed else 0,)), ((), ()))
    count = rows.shape[0]
    high, low = split(rows)
    both = lax.dot_general(
        jnp.concatenate([high, low], axis=0), w_high, dims, preferred_element_type=F32
    )
    rest = lax.dot_general(high, w_low, dims, preferred_element_type=F32)
    return both[:count] + both[count:] + rest


def cg_kernel(
    n, snps, chunks,
    gh, gl, kh, kl, x_in, r_in, p_in, ratio_in,
    x_out, r_out, p_out,
    part0, rs0, ag0, part, rs, ag, sums_ref, u_ref, image_ref,
    rs_send, rs_recv, ag_send, ag_recv,
):
    me = lax.axis_index("ind")
    people = x_in.shape[1]
    traits = x_in.shape[0]
    owners = [(c * n) // chunks for c in range(chunks)]
    mine = (me * chunks + n - 1) // n
    is_owner = jnp.logical_and((mine * n) // chunks == me, mine < chunks)
    mine = jnp.minimum(mine, chunks - 1)

    barrier = pltpu.get_barrier_semaphore()

    @pl.when(is_owner)
    def _():
        @pl.loop(1, n)
        def _(j):
            pl.semaphore_signal(
                barrier, inc=1, device_id={"ind": lax.rem(me + j, n)},
                device_id_type=pl.DeviceIdType.MESH,
            )

        pl.semaphore_wait(barrier, n - 1)

    @pl.when(jnp.logical_not(is_owner))
    def _():
        for o in owners:
            pl.semaphore_signal(
                barrier, inc=1, device_id={"ind": o},
                device_id_type=pl.DeviceIdType.MESH,
            )
        pl.semaphore_wait(barrier, chunks)

    def scatter_start(src, dst, which):
        for c, o in enumerate(owners):
            @pl.when(me != o)
            def _():
                pltpu.make_async_remote_copy(
                    src_ref=src.at[c], dst_ref=dst.at[lax.rem(me - o - 1 + n, n)],
                    send_sem=rs_send.at[which], recv_sem=rs_recv.at[which],
                    device_id={"ind": o}, device_id_type=pl.DeviceIdType.MESH,
                ).start()

    def local(src, dst, send, recv):
        return pltpu.make_async_remote_copy(
            src_ref=src, dst_ref=dst, send_sem=send, recv_sem=recv,
            device_id={"ind": lax.rem(me + 1, n)},
            device_id_type=pl.DeviceIdType.MESH,
        )

    def sum_and_gather(src, buf, out, which):
        @pl.when(is_owner)
        def _():
            local(buf, buf, rs_send.at[which], rs_recv.at[which]).wait_recv()
            out[mine] = src[mine] + jnp.sum(buf[...], axis=0)

            @pl.loop(1, n)
            def _(j):
                pltpu.make_async_remote_copy(
                    src_ref=out.at[mine], dst_ref=out.at[mine],
                    send_sem=ag_send.at[which], recv_sem=ag_recv.at[which],
                    device_id={"ind": lax.rem(me + j, n)},
                    device_id_type=pl.DeviceIdType.MESH,
                ).start()

    def finish(src, buf, out, which):
        @pl.when(is_owner)
        def _():
            few = out.at[pl.ds(0, chunks - 1)]
            local(few, few, ag_send.at[which], ag_recv.at[which]).wait_recv()
            few = src.at[pl.ds(0, chunks - 1)]
            local(few, few, rs_send.at[which], rs_recv.at[which]).wait_send()
            local(buf, buf, ag_send.at[which], ag_recv.at[which]).wait_send()

        @pl.when(jnp.logical_not(is_owner))
        def _():
            local(out, out, ag_send.at[which], ag_recv.at[which]).wait_recv()
            local(src, src, rs_send.at[which], rs_recv.at[which]).wait_send()

    def put(dst, value):
        for c in range(chunks):
            dst[c] = value[:, c * LANES:(c + 1) * LANES]

    def whole(src):
        return jnp.concatenate([src[c] for c in range(chunks)], axis=1)

    wide = lax.broadcasted_iota(jnp.int32, (1, chunks * LANES), 1)
    real = wide < snps

    put(part0, product(jnp.concatenate([p_in[...], r_in[...]], axis=0), gh[...], gl[...]))
    scatter_start(part0, rs0, 0)
    x_out[...] = x_in[...]
    r_out[...] = r_in[...]
    p_out[...] = p_in[...]
    sum_and_gather(part0, rs0, ag0, 0)
    finish(part0, rs0, ag0, 0)
    start = whole(ag0)
    sums_ref[...] = start[:traits]
    u_ref[...] = start[traits:]
    ratio = ratio_in[...]
    scale = 1.0 / snps
    half = people // 2

    def image_half(s, i):
        cut = pl.ds(i * half, half)
        image_ref[:, cut] = (
            product(s, gh[cut, :], gl[cut, :], True) / snps + ratio * p_out[:, cut]
        )

    @pl.loop(0, ITERS)
    def _(step):
        s = sums_ref[...]
        t = product(s, kh[...], kl[...])
        r, p = r_out[...], p_out[...]
        rr = jnp.sum(r * r, axis=1, keepdims=True)
        rp = jnp.sum(r * p, axis=1, keepdims=True)
        pp = jnp.sum(p * p, axis=1, keepdims=True)
        t = t + jnp.where(
            wide == snps, rr,
            jnp.where(wide == snps + 1, rp, jnp.where(wide == snps + 2, pp, 0.0)),
        )
        put(part, t)
        scatter_start(part, rs, 1)
        image_half(s, 0)
        sum_and_gather(part, rs, ag, 1)
        image_half(s, 1)
        finish(part, rs, ag, 1)

        t = whole(ag)
        rr = t[:, snps:snps + 1]
        rp = t[:, snps + 1:snps + 2]
        pp = t[:, snps + 2:snps + 3]
        t = jnp.where(real, t, 0.0)
        u = u_ref[...]
        ss = jnp.sum(s * s, axis=1, keepdims=True) * scale
        us = jnp.sum(u * s, axis=1, keepdims=True) * scale
        ts = jnp.sum(t * s, axis=1, keepdims=True) * (scale * scale)
        alpha = rr / (ss + ratio * pp)
        cross = us + ratio * rp
        norm = ts + ratio * (2.0 * ss + ratio * pp)
        fresh = rr - alpha * (2.0 * cross - alpha * norm)
        beta = fresh / rr
        u = u - alpha * (t * scale + ratio * s)
        u_ref[...] = u
        sums_ref[...] = u + beta * s
        p = p_out[...]
        x_out[...] = x_out[...] + alpha * p
        r = r_out[...] - alpha * image_ref[...]
        r_out[...] = r
        p_out[...] = r + beta * p


def per_device(n, genotypes, solution, residual, direction, ratio):
    people, snps = genotypes.shape
    traits = solution.shape[0]
    chunks = -(-(snps + 3) // LANES)
    padded = chunks * LANES
    g = jnp.pad(genotypes, ((0, 0), (0, padded - snps)))
    high = lax.reduce_precision(g, 8, 7)
    gh = high.astype(BF16)
    gl = (g - high).astype(BF16)
    dims = (((0,), (0,)), ((), ()))
    hh = lax.dot_general(gh, gh, dims, preferred_element_type=F32)
    hl = lax.dot_general(gh, gl, dims, preferred_element_type=F32)
    gram = hh + hl + hl.T
    k_high = lax.reduce_precision(gram, 8, 7)
    kh = k_high.astype(BF16)
    kl = (gram - k_high).astype(BF16)

    vmem = pl.BlockSpec(memory_space=pltpu.VMEM)
    shape = jax.ShapeDtypeStruct((traits, people), F32)
    return pl.pallas_call(
        functools.partial(cg_kernel, n, snps, chunks),
        out_shape=(shape, shape, shape),
        in_specs=[vmem] * 8,
        out_specs=(vmem, vmem, vmem),
        scratch_shapes=[
            pltpu.VMEM((chunks, 2 * traits, LANES), F32),
            pltpu.VMEM((n - 1, 2 * traits, LANES), F32),
            pltpu.VMEM((chunks, 2 * traits, LANES), F32),
            pltpu.VMEM((chunks, traits, LANES), F32),
            pltpu.VMEM((n - 1, traits, LANES), F32),
            pltpu.VMEM((chunks, traits, LANES), F32),
            pltpu.VMEM((traits, padded), F32),
            pltpu.VMEM((traits, padded), F32),
            pltpu.VMEM((traits, people), F32),
            pltpu.SemaphoreType.DMA((2,)),
            pltpu.SemaphoreType.DMA((2,)),
            pltpu.SemaphoreType.DMA((2,)),
            pltpu.SemaphoreType.DMA((2,)),
        ],
        compiler_params=pltpu.CompilerParams(
            collective_id=0, has_side_effects=True, vmem_limit_bytes=56 * 2**20
        ),
    )(gh, gl, kh, kl, solution, residual, direction, ratio[:, None])


def solution(mesh):
    cols = P(None, ("cohort", "ind"))
    return jax.shard_map(
        functools.partial(per_device, mesh.shape["ind"]),
        mesh=mesh,
        in_specs=(P(("cohort", "ind"), None), cols, cols, cols, P("cohort")),
        out_specs=(cols, cols, cols),
        check_vma=False,
    )
```

time: 1340 us -> 175 us (0.13)
  waiting for transfers between devices: 665 us -> 0 us
  blocking collectives: 496 us -> 0 us
  matrix products: 150 us -> 27.9 us
  Pallas kernels: 0 us -> 112 us
  local copies, waits for them, and re-layouts: 0.02 us -> 24.7 us
  between operations: 14.8 us -> 0.64 us
    psum x8 -> x0, waiting for transfers between devices: 665 us -> none  [sum_over_people(): return lax.psum(values, 'ind')]
    psum x16 -> x0, blocking collectives: 496 us -> none  [the longest x9 269 us: squares(): return lax.psum(jnp.sum(residual * residual, axis=1), 'ind')]
    dot_general x16 -> x2, matrix products: 150 us -> 27.9 us  [the longest x1 15.6 us: per_device(): hh = lax.dot_general(gh, gh, dims, preferred_element_type=F32)]
    pallas_call x0 -> x1, Pallas kernels: none -> 112 us  [per_device(): pl.pallas_call(functools.partial(cg_kernel, n, snps, chunks), out_shape=(...]
    unnamed x10 -> x6, local copies, waits for them, and re-layouts: 0.02 us -> 15.8 us
  transfers between devices with their start and end apart: 8 -> 0, of which waited for: 8 -> 0; matrix products, arithmetic and copies ran while one was open for 0% -> 0% of each run, Pallas kernels for 0% -> 0%
where the time goes in v1:
time: 175 us
  Pallas kernels  112 us (64%)
  matrix products  27.9 us (16%)
  local copies, waits for them, and re-layouts  24.7 us (14%)
  other arithmetic  9.39 us (5%)
    pallas_call x1, Pallas kernels, per_device(): pl.pallas_call(functools.partial(cg_kernel, n, snps, chunks), out_shape=(...  112 us
    unnamed x6, local copies, waits for them, and re-layouts  15.8 us
    dot_general x1, matrix products, per_device(): hh = lax.dot_general(gh, gh, dims, preferred_element_type=F32)  15.6 us
    dot_general x1, matrix products, per_device(): hl = lax.dot_general(gh, gl, dims, preferred_element_type=F32)  12.3 us
    convert_element_type x1, other arithmetic, per_device(): gl = (g - high).astype(BF16)  9.39 us
    dot_general x1, local copies, waits for them, and re-layouts, per_device(): hl = lax.dot_general(gh, gl, dims, preferred_element_type=F32)  8.18 us

profile of v1, /device:TPU:0, one launch (start us, length us, event | category | flops | bytes accessed | tf_op | source)
XLA Modules:
  0.0 174.7 jit_solution(420546025217892436)
XLA Ops:
  0.6 11.1 %copy.8 = f32[2048,1200]{1,0:T(8,128)} copy(f32[2048,1200]{0,1:T(8,128)} %param.5) | data formatting | bytes 19660800 | tf_op args[0]
  11.7 9.4 %fusion = (bf16[2048,1280]{1,0:T(8,128)(2,1)}, bf16[2048,1280]{1,0:T(8,128)(2,1)}) fusion(f32[2048,1200]{1,0:T(8,128)} %copy.8), kind=kLoop, calls=%fused_computation.2 | loop fusion | flops 10485760 | bytes 20316160 | tf_op jit(solution)/shard_map/convert_element_type | solution.py:197
  21.1 12.3 %fusion.3 = f32[1280,1280]{1,0:T(8,128)} fusion(bf16[2048,1280]{1,0:T(8,128)(2,1)} %get-tuple-element.4.gh, bf16[2048,1280]{1,0:T(8,128)(2,1)} %get-tuple-element.3.gl), kind=kOutput, calls=%fused_computation.8 | convolution fusion | flops 6710886400 | bytes 17039360 | tf_op jit(solution)/shard_map/dot_general | solution.py:200
  33.4 8.2 %copy.9 = f32[1280,1280]{0,1:T(8,128)} copy(f32[1280,1280]{1,0:T(8,128)} %fusion.3) | data formatting | bytes 13107200 | tf_op jit(solution)/shard_map/dot_general | solution.py:200
  41.6 0.0 copy-start
  41.6 15.6 %fusion.2 = (bf16[1280,1280]{1,0:T(8,128)(2,1)}, bf16[1280,1280]{1,0:T(8,128)(2,1)}) fusion(f32[1280,1280]{0,1:T(8,128)} %copy.9, f32[1280,1280]{1,0:T(8,128)} %fusion.3, bf16[2048,1280]{1,0:T(8,128)(2,1)} %get-tuple-element.4.gh), kind=kOutput, calls=%fused_computation.7 | convolution fusion | flops 6720716800 | bytes 24903680 | tf_op jit(solution)/shard_map/dot_general | solution.py:199
  57.2 0.0 copy-done
  57.2 0.7 copy.10.ratio_in
  57.9 112.2 %shard_map.76 = (f32[16,2048]{1,0:T(8,128)}, f32[16,2048]{1,0:T(8,128)}, f32[16,2048]{1,0:T(8,128)}) custom-call(bf16[2048,1280]{1,0:T(8,128)(2,1)} %get-tuple-element.4.gh, bf16[2048,1280]{1,0:T(8,128)(2,1)} %get-tuple-element.3.gl, bf16[1280,1280]{1,0:T(8,128)(2,1)} %get-tuple-element.6.kh, bf16[1280,1280]{1,0:T(8,128)(2,1)} %get-tuple-element.5.kl, ...), custom_call_target="tpu_custom_call" | custom-call | tf_op jit(solution)/shard_map/pallas_call | solution.py:208
  170.0 1.6 copy.14
  171.6 1.6 copy.15
  173.2 1.6 copy.16
Async XLA Ops:
  41.6 15.6 %copy-start = (f32[16]{0:T(128)S(1)}, f32[16]{0:T(128)}, u32[]{:S(2)}) copy-start(f32[16]{0:T(128)} %param.9) | copy-start | bytes 196

commit v2 on v1

--- a/solution.py
+++ b/solution.py
@@ -9,6 +9,7 @@
 
 ITERS = 8
 LANES = 128
+ROWS = 256
 F32 = jnp.float32
 BF16 = jnp.bfloat16
 
@@ -19,8 +20,8 @@
     return high, low
 
 
-def product(rows, w_high, w_low, transposed=False):
-    dims = (((1,), (1 if transposed else 0,)), ((), ()))
+def product(rows, w_high, w_low):
+    dims = (((1,), (0,)), ((), ()))
     count = rows.shape[0]
     high, low = split(rows)
     both = lax.dot_general(
@@ -32,9 +33,9 @@
 
 def cg_kernel(
     n, snps, chunks,
-    gh, gl, kh, kl, x_in, r_in, p_in, ratio_in,
+    g_in, x_in, r_in, p_in, ratio_in,
     x_out, r_out, p_out,
-    part0, rs0, ag0, part, rs, ag, sums_ref, u_ref, image_ref,
+    raw, gh, gl, th, tl, kh, kl, g_sem, first, part0, rs0, ag0, part, rs, ag, sums_ref, u_ref, image_ref,
     rs_send, rs_recv, ag_send, ag_recv,
 ):
     me = lax.axis_index("ind")
@@ -45,6 +46,17 @@
     is_owner = jnp.logical_and((mine * n) // chunks == me, mine < chunks)
     mine = jnp.minimum(mine, chunks - 1)
 
+    rows = ROWS if people % ROWS == 0 else people
+    steps = people // rows
+    tail = (chunks - 1) * LANES
+
+    def load(i):
+        cut = pl.ds(pl.multiple_of(i * rows, rows), rows)
+        return pltpu.make_async_copy(g_in.at[cut], raw.at[cut], g_sem.at[i])
+
+    for i in range(steps):
+        load(i).start()
+
     barrier = pltpu.get_barrier_semaphore()
 
     @pl.when(is_owner)
@@ -123,12 +135,53 @@
     wide = lax.broadcasted_iota(jnp.int32, (1, chunks * LANES), 1)
     real = wide < snps
 
-    put(part0, product(jnp.concatenate([p_in[...], r_in[...]], axis=0), gh[...], gl[...]))
+    gh[:, tail:] = jnp.zeros((people, LANES), BF16)
+    gl[:, tail:] = jnp.zeros((people, LANES), BF16)
+    first[...] = jnp.zeros_like(first)
+
+    @pl.loop(0, steps)
+    def _(i):
+        load(i).wait()
+        cut = pl.ds(pl.multiple_of(i * rows, rows), rows)
+        for c in range(chunks):
+            lanes = slice(c * LANES, min((c + 1) * LANES, snps))
+            high, low = split(raw[cut, lanes])
+            gh[cut, lanes] = high
+            gl[cut, lanes] = low
+        both = jnp.concatenate([p_in[:, cut], r_in[:, cut]], axis=0)
+        first[...] += product(both, gh[cut, :], gl[cut, :])
+
+    put(part0, first[...])
     scatter_start(part0, rs0, 0)
     x_out[...] = x_in[...]
     r_out[...] = r_in[...]
     p_out[...] = p_in[...]
+
+    @pl.loop(0, steps)
+    def _(i):
+        cut = pl.ds(pl.multiple_of(i * rows, rows), rows)
+        th[:, cut] = gh[cut, :].T
+        tl[:, cut] = gl[cut, :].T
+
     sum_and_gather(part0, rs0, ag0, 0)
+
+    width = 2 * LANES
+    for j in range(chunks // 2):
+        lanes = slice(j * width, (j + 1) * width)
+        top = (j + 1) * width
+        block = (
+            jnp.dot(th[:top], gh[:, lanes], preferred_element_type=F32)
+            + jnp.dot(th[:top], gl[:, lanes], preferred_element_type=F32)
+            + jnp.dot(tl[:top], gh[:, lanes], preferred_element_type=F32)
+        )
+        high, low = split(block)
+        kh[:top, lanes] = high
+        kl[:top, lanes] = low
+        for i in range(j):
+            under = slice(i * width, (i + 1) * width)
+            kh[lanes, under] = high[under].T
+            kl[lanes, under] = low[under].T
+
     finish(part0, rs0, ag0, 0)
     start = whole(ag0)
     sums_ref[...] = start[:traits]
@@ -140,7 +193,7 @@
     def image_half(s, i):
         cut = pl.ds(i * half, half)
         image_ref[:, cut] = (
-            product(s, gh[cut, :], gl[cut, :], True) / snps + ratio * p_out[:, cut]
+            product(s, th[:, cut], tl[:, cut]) * scale + ratio * p_out[:, cut]
         )
 
     @pl.loop(0, ITERS)
@@ -190,27 +243,27 @@
     people, snps = genotypes.shape
     traits = solution.shape[0]
     chunks = -(-(snps + 3) // LANES)
+    chunks += chunks % 2
     padded = chunks * LANES
-    g = jnp.pad(genotypes, ((0, 0), (0, padded - snps)))
-    high = lax.reduce_precision(g, 8, 7)
-    gh = high.astype(BF16)
-    gl = (g - high).astype(BF16)
-    dims = (((0,), (0,)), ((), ()))
-    hh = lax.dot_general(gh, gh, dims, preferred_element_type=F32)
-    hl = lax.dot_general(gh, gl, dims, preferred_element_type=F32)
-    gram = hh + hl + hl.T
-    k_high = lax.reduce_precision(gram, 8, 7)
-    kh = k_high.astype(BF16)
-    kl = (gram - k_high).astype(BF16)
+    rows = ROWS if people % ROWS == 0 else people
 
     vmem = pl.BlockSpec(memory_space=pltpu.VMEM)
     shape = jax.ShapeDtypeStruct((traits, people), F32)
     return pl.pallas_call(
         functools.partial(cg_kernel, n, snps, chunks),
         out_shape=(shape, shape, shape),
-        in_specs=[vmem] * 8,
+        in_specs=[pl.BlockSpec(memory_space=pl.ANY)] + [vmem] * 4,
         out_specs=(vmem, vmem, vmem),
         scratch_shapes=[
+            pltpu.VMEM((people, snps), F32),
+            pltpu.VMEM((people, padded), BF16),
+            pltpu.VMEM((people, padded), BF16),
+            pltpu.VMEM((padded, people), BF16),
+            pltpu.VMEM((padded, people), BF16),
+            pltpu.VMEM((padded, padded), BF16),
+            pltpu.VMEM((padded, padded), BF16),
+            pltpu.SemaphoreType.DMA((people // rows,)),
+            pltpu.VMEM((2 * traits, padded), F32),
             pltpu.VMEM((chunks, 2 * traits, LANES), F32),
             pltpu.VMEM((n - 1, 2 * traits, LANES), F32),
             pltpu.VMEM((chunks, 2 * traits, LANES), F32),
@@ -228,7 +281,7 @@
         compiler_params=pltpu.CompilerParams(
             collective_id=0, has_side_effects=True, vmem_limit_bytes=56 * 2**20
         ),
-    )(gh, gl, kh, kl, solution, residual, direction, ratio[:, None])
+    )(genotypes, solution, residual, direction, ratio[:, None])
 
 
 def solution(mesh):

time: 175 us -> 133 us (0.76)
  matrix products: 27.9 us -> 0 us
  other arithmetic: 9.39 us -> 0 us
  local copies, waits for them, and re-layouts: 24.7 us -> 17.2 us
  Pallas kernels: 112 us -> 115 us
    dot_general x2 -> x0, matrix products: 27.9 us -> none  [the longest x1 15.6 us: per_device(): hh = lax.dot_general(gh, gh, dims, preferred_element_type=F32)]
    convert_element_type x1 -> x0, other arithmetic: 9.39 us -> none  [per_device(): gl = (g - high).astype(BF16)]
    dot_general x1 -> x0, local copies, waits for them, and re-layouts: 8.18 us -> none  [per_device(): hl = lax.dot_general(gh, gl, dims, preferred_element_type=F32)]
    pallas_call x1, Pallas kernels: 112 us -> 115 us  [per_device(): pl.pallas_call(functools.partial(cg_kernel, n, snps, chunks), out_shape=(...]
    unnamed x6 -> x4, local copies, waits for them, and re-layouts: 15.8 us -> 15.8 us
where the time goes in v2:
time: 133 us
  Pallas kernels  115 us (86%)
  local copies, waits for them, and re-layouts  17.2 us (13%)
    pallas_call x1, Pallas kernels, per_device(): pl.pallas_call(functools.partial(cg_kernel, n, snps, chunks), out_shape=(...  115 us
    unnamed x4, local copies, waits for them, and re-layouts  15.8 us

profile of v2, /device:TPU:0, one launch (start us, length us, event | category | flops | bytes accessed | tf_op | source)
XLA Modules:
  0.0 133.0 jit_solution(2815357985600891164)
XLA Ops:
  0.6 1.3 copy.9.ratio_in
  2.0 11.1 %copy.8.g_in = f32[2048,1200]{1,0:T(8,128)} copy(f32[2048,1200]{0,1:T(8,128)} %param.5) | data formatting | bytes 19660800 | tf_op args[0]
  13.1 115.2 %shard_map.76 = (f32[16,2048]{1,0:T(8,128)}, f32[16,2048]{1,0:T(8,128)}, f32[16,2048]{1,0:T(8,128)}) custom-call(f32[2048,1200]{1,0:T(8,128)} %copy.8.g_in, f32[16,2048]{1,0:T(8,128)} %x_in.1, f32[16,2048]{1,0:T(8,128)} %r_in.1, f32[16,2048]{1,0:T(8,128)} %p_in.1, f32[16,1]{1,0:T(8,128)} %copy.9.ratio_in), custom_call_target="tpu_custom_call" | custom-call | tf_op jit(solution)/shard_map/pallas_call | solution.py:252
  128.3 1.6 %copy.13 = f32[16,2048]{1,0:T(8,128)} copy(f32[16,2048]{1,0:T(8,128)} %get-tuple-element.6) | data formatting | bytes 262144
  129.9 1.6 %copy.14 = f32[16,2048]{1,0:T(8,128)} copy(f32[16,2048]{1,0:T(8,128)} %get-tuple-element.7) | data formatting | bytes 262144
  131.5 1.6 %copy.15 = f32[16,2048]{1,0:T(8,128)} copy(f32[16,2048]{1,0:T(8,128)} %get-tuple-element.8) | data formatting | bytes 262144

commit v3 on v2

--- a/solution.py
+++ b/solution.py
@@ -35,13 +35,12 @@
     n, snps, chunks,
     g_in, x_in, r_in, p_in, ratio_in,
     x_out, r_out, p_out,
-    raw, gh, gl, th, tl, kh, kl, g_sem, first, part0, rs0, ag0, part, rs, ag, sums_ref, u_ref, image_ref,
+    raw, gh, gl, th, tl, kh, kl, g_sem, first, part0, rs0, ag0, part, rs, ag, sums_ref, u_ref, image_ref, scalars, last,
     rs_send, rs_recv, ag_send, ag_recv,
 ):
     me = lax.axis_index("ind")
     people = x_in.shape[1]
     traits = x_in.shape[0]
-    owners = [(c * n) // chunks for c in range(chunks)]
     mine = (me * chunks + n - 1) // n
     is_owner = jnp.logical_and((mine * n) // chunks == me, mine < chunks)
     mine = jnp.minimum(mine, chunks - 1)
@@ -59,28 +58,19 @@
 
     barrier = pltpu.get_barrier_semaphore()
 
-    @pl.when(is_owner)
-    def _():
-        @pl.loop(1, n)
-        def _(j):
-            pl.semaphore_signal(
-                barrier, inc=1, device_id={"ind": lax.rem(me + j, n)},
-                device_id_type=pl.DeviceIdType.MESH,
-            )
-
-        pl.semaphore_wait(barrier, n - 1)
-
-    @pl.when(jnp.logical_not(is_owner))
-    def _():
-        for o in owners:
-            pl.semaphore_signal(
-                barrier, inc=1, device_id={"ind": o},
-                device_id_type=pl.DeviceIdType.MESH,
-            )
-        pl.semaphore_wait(barrier, chunks)
+    @pl.loop(1, n)
+    def _(j):
+        pl.semaphore_signal(
+            barrier, inc=1, device_id={"ind": lax.rem(me + j, n)},
+            device_id_type=pl.DeviceIdType.MESH,
+        )
+
+    pl.semaphore_wait(barrier, n - 1)
 
     def scatter_start(src, dst, which):
-        for c, o in enumerate(owners):
+        for c in range(chunks):
+            o = (c * n) // chunks
+
             @pl.when(me != o)
             def _():
                 pltpu.make_async_remote_copy(
@@ -196,7 +186,7 @@
             product(s, th[:, cut], tl[:, cut]) * scale + ratio * p_out[:, cut]
         )
 
-    @pl.loop(0, ITERS)
+    @pl.loop(0, ITERS - 1)
     def _(step):
         s = sums_ref[...]
         t = product(s, kh[...], kl[...])
@@ -233,10 +223,41 @@
         u_ref[...] = u
         sums_ref[...] = u + beta * s
         p = p_out[...]
+        scalars[0] = jnp.broadcast_to(fresh, scalars.shape[1:])
+        scalars[1] = jnp.broadcast_to(
+            fresh + beta * (2.0 * (rp - rr) + beta * pp), scalars.shape[1:]
+        )
         x_out[...] = x_out[...] + alpha * p
         r = r_out[...] - alpha * image_ref[...]
         r_out[...] = r
         p_out[...] = r + beta * p
+
+    s = sums_ref[...]
+    image_half(s, 0)
+    image_half(s, 1)
+    ss = jnp.sum(s * s, axis=1, keepdims=True) * scale
+    alpha = scalars[0][:, :1] / (ss + ratio * scalars[1][:, :1])
+    r, p = r_out[...], p_out[...]
+    before = jnp.sum(r * r, axis=1, keepdims=True)
+    r = r - alpha * image_ref[...]
+    fresh = jnp.sum(r * r, axis=1, keepdims=True)
+    lane = lax.broadcasted_iota(jnp.int32, scalars.shape[1:], 1)
+    scalars[2] = jnp.where(lane == 0, before, fresh)
+
+    @pl.loop(1, n)
+    def _(j):
+        pltpu.make_async_remote_copy(
+            src_ref=scalars.at[2], dst_ref=last.at[n - 1 - j],
+            send_sem=rs_send.at[2], recv_sem=rs_recv.at[2],
+            device_id={"ind": lax.rem(me + j, n)},
+            device_id_type=pl.DeviceIdType.MESH,
+        ).start()
+
+    r_out[...] = r
+    x_out[...] = x_out[...] + alpha * p
+    local(last, last, rs_send.at[2], rs_recv.at[2]).wait()
+    both = scalars[2] + jnp.sum(last[...], axis=0)
+    p_out[...] = r + (both[:, 1:2] / both[:, :1]) * p
 
 
 def per_device(n, genotypes, solution, residual, direction, ratio):
@@ -273,8 +294,10 @@
             pltpu.VMEM((traits, padded), F32),
             pltpu.VMEM((traits, padded), F32),
             pltpu.VMEM((traits, people), F32),
-            pltpu.SemaphoreType.DMA((2,)),
-            pltpu.SemaphoreType.DMA((2,)),
+            pltpu.VMEM((3, traits, LANES), F32),
+            pltpu.VMEM((n - 1, traits, LANES), F32),
+            pltpu.SemaphoreType.DMA((3,)),
+            pltpu.SemaphoreType.DMA((3,)),
             pltpu.SemaphoreType.DMA((2,)),
             pltpu.SemaphoreType.DMA((2,)),
         ],

time: 133 us -> 132 us (level)
  Pallas kernels: 115 us -> 113 us
    pallas_call x1, Pallas kernels: 115 us -> 113 us  [per_device(): pl.pallas_call(functools.partial(cg_kernel, n, snps, chunks), out_shape=(...]
where the time goes in v3:
time: 132 us; the launch traced here: 131 us
  Pallas kernels  113 us (86%)
  local copies, waits for them, and re-layouts  17.2 us (13%)
    pallas_call x1, Pallas kernels, per_device(): pl.pallas_call(functools.partial(cg_kernel, n, snps, chunks), out_shape=(...  113 us
    unnamed x4, local copies, waits for them, and re-layouts  15.8 us

profile of v3, /device:TPU:0, one launch (start us, length us, event | category | flops | bytes accessed | tf_op | source)
XLA Modules:
  0.0 131.2 jit_solution(4801399528810439188)
XLA Ops:
  0.6 1.3 %copy.9.ratio_in = f32[16,1]{1,0:T(8,128)} copy(f32[16,1]{0,1:T(1,128)} %bitcast.1) | data formatting | bytes 128 | tf_op jit(solution)/shard_map/broadcast_in_dim | solution.py:307
  2.0 11.1 %copy.8.g_in = f32[2048,1200]{1,0:T(8,128)} copy(f32[2048,1200]{0,1:T(8,128)} %param.5) | data formatting | bytes 19660800 | tf_op args[0]
  13.1 113.4 %shard_map.76 = (f32[16,2048]{1,0:T(8,128)}, f32[16,2048]{1,0:T(8,128)}, f32[16,2048]{1,0:T(8,128)}) custom-call(f32[2048,1200]{1,0:T(8,128)} %copy.8.g_in, f32[16,2048]{1,0:T(8,128)} %x_in.1, f32[16,2048]{1,0:T(8,128)} %r_in.1, f32[16,2048]{1,0:T(8,128)} %p_in.1, f32[16,1]{1,0:T(8,128)} %copy.9.ratio_in), custom_call_target="tpu_custom_call" | custom-call | tf_op jit(solution)/shard_map/pallas_call | solution.py:273
  126.5 1.6 %copy.13 = f32[16,2048]{1,0:T(8,128)} copy(f32[16,2048]{1,0:T(8,128)} %get-tuple-element.6) | data formatting | bytes 262144
  128.0 1.6 %copy.14 = f32[16,2048]{1,0:T(8,128)} copy(f32[16,2048]{1,0:T(8,128)} %get-tuple-element.7) | data formatting | bytes 262144
  129.6 1.6 %copy.15 = f32[16,2048]{1,0:T(8,128)} copy(f32[16,2048]{1,0:T(8,128)} %get-tuple-element.8) | data formatting | bytes 262144
